TPU v7x, 256 devices: a whole 4x4x8 slice. The times are simulated.
256 devices in a mesh: dp: 32 (over z, x), fsdp: 8 (over y, core).
Axes of the slice: x: 4, y: 4, z: 8, core: 2. Of those that a mesh axis runs over, the one named last changes fastest.
Arguments:
- incoming_feature_maps: bfloat16 [256, 8, 8, 3072], P('dp', None, None, 'fsdp'), may hold values from -6 to 6
- spatial_filter_tensor: bfloat16 [7, 7, 3072], P(None, None, 'fsdp'), may hold values from -0.875 to 0.875
- spatial_filter_offset: float32 [3072], P('fsdp'), may hold values from -3 to 3
- unit_layernorm_multiplier: float32 [3072], replicated, may hold values from 0.5 to 1.5
- unit_layernorm_offset_vector: float32 [3072], replicated, may hold values from -3 to 3
- expansion_linear_map: bfloat16 [3072, 12288], P('dp', 'fsdp'), may hold values from -0.109375 to 0.109375
- expansion_offset: float32 [12288], P('fsdp'), may hold values from -3 to 3
- contraction_linear_map: bfloat16 [12288, 3072], P('fsdp', 'dp'), may hold values from -0.109375 to 0.109375
- contraction_offset: float32 [3072], P('fsdp'), may hold values from -3 to 3
- residual_channel_factor: float32 [3072], P('fsdp'), may hold values from 0.3 to 1.5
- readout_layernorm_multiplier: float32 [3072], P('fsdp'), may hold values from 0.5 to 1.5
- readout_layernorm_offset: float32 [3072], P('fsdp'), may hold values from -3 to 3
- readout_linear_map: bfloat16 [3072, 768], P('fsdp'), may hold values from -0.109375 to 0.109375
- learner_caption_vectors: bfloat16 [16384, 768], P(('dp', 'fsdp')), may hold values from -6 to 6
- mentor_caption_vectors: bfloat16 [16384, 768], P(('dp', 'fsdp')), may hold values from -6 to 6
- mentor_picture_vectors: bfloat16 [256, 768], P('dp'), may hold values from -6 to 6
- divisor_per_slot: float32 [64], replicated, may hold values from 0.003 to 0.07
- active_program_slot: int32 [1], replicated, may hold values from 0 to 63
- matching_caption_slot: int32 [256], replicated, may hold values from 0 to 16383
Outputs:
- block_out: bfloat16 [256, 8, 8, 3072], P('dp', None, None, 'fsdp')
- embedding: float32 [256, 768], P('dp')
- losses: float32 [256], P(('dp', 'fsdp'))
All inputs are finite; a program needn't handle non-finite values.
Results may differ from a plain program's by a relative error of at most 0.015.
Values may be sent and summed in bfloat16 or wider, within the bound.
No kernel may reach another device: no remote copies, remote signals or barrier semaphores. Data moves between devices by JAX's collectives and lax.ppermute only.
A program may use at most 128 MiB of HBM per device.

v0:
```python
import jax
import jax.numpy as jnp
from jax import lax
from jax.sharding import PartitionSpec as P

SIDE = 8
KERNEL = 7


EPSILON = 1e-06
HIGHEST = lax.Precision.HIGHEST


def combined_all(value, axis, join):
    pieces = jax.tree.map(lambda part: lax.all_gather(part, axis), value)
    head = jax.tree.map(lambda part: part[0], pieces)
    tail = jax.tree.map(lambda part: part[1:], pieces)
    so_far, _ = lax.scan(lambda so_far, share: (join(so_far, share), None), head, tail)
    return so_far


def depthwise(incoming_feature_maps, spatial_filter_tensor, spatial_filter_offset):
    radius = KERNEL // 2
    padded = jnp.pad(
        incoming_feature_maps.astype(jnp.float32),
        ((0, 0), (radius, radius), (radius, radius), (0, 0)),
    )
    summed = jnp.zeros(incoming_feature_maps.shape, jnp.float32)
    for vertical in range(KERNEL):
        for horizontal in range(KERNEL):
            window = padded[:, vertical : vertical + SIDE, horizontal : horizontal + SIDE, :]
            summed = (
                summed + spatial_filter_tensor[vertical, horizontal].astype(jnp.float32) * window
            )
    return (summed + spatial_filter_offset).astype(jnp.bfloat16)


def unit_rows(values):
    return (values / jnp.sqrt(jnp.sum(values * values, -1, keepdims=True) + EPSILON)).astype(
        jnp.bfloat16
    )


def matching_logit_entries(queries, keys_block):
    return lax.dot_general(
        queries, keys_block, (((1,), (1,)), ((), ())), preferred_element_type=jnp.float32
    )


def row_stats(
    learner_picture_vectors,
    mentor_picture_list,
    learner_caption_tile,
    mentor_caption_tile,
    target_affinity,
    first_column_index,
    logit_divisor,
):
    learner_network = (
        matching_logit_entries(learner_picture_vectors, learner_caption_tile) / logit_divisor
    )
    mentor_network = (
        matching_logit_entries(mentor_picture_list, mentor_caption_tile) / logit_divisor
    )
    top_student = jnp.max(learner_network, 1)
    top_teacher = jnp.max(mentor_network, 1)
    weights_student = jnp.exp(learner_network - top_student[:, None])
    weights_teacher = jnp.exp(mentor_network - top_teacher[:, None])
    column_ids = first_column_index + lax.iota(jnp.int32, learner_caption_tile.shape[0])
    label_score = jnp.sum(
        jnp.where(target_affinity[:, None] == column_ids[None, :], learner_network, 0.0), 1
    )
    cross_sum = jnp.sum(weights_teacher * (mentor_network - learner_network), 1)
    return (
        top_student,
        jnp.sum(weights_student, 1),
        top_teacher,
        jnp.sum(weights_teacher, 1),
        cross_sum,
        label_score,
    )


def combine_stats(former, latter):
    top_student = jnp.maximum(former[0], latter[0])
    former_student = jnp.exp(former[0] - top_student)
    latter_student = jnp.exp(latter[0] - top_student)
    top_teacher = jnp.maximum(former[2], latter[2])
    former_teacher = jnp.exp(former[2] - top_teacher)
    latter_teacher = jnp.exp(latter[2] - top_teacher)
    return (
        top_student,
        former[1] * former_student + latter[1] * latter_student,
        top_teacher,
        former[3] * former_teacher + latter[3] * latter_teacher,
        former[4] * former_teacher + latter[4] * latter_teacher,
        former[5] + latter[5],
    )


def on_device(
    incoming_feature_maps,
    spatial_filter_tensor,
    spatial_filter_offset,
    unit_layernorm_multiplier,
    unit_layernorm_offset_vector,
    expansion_linear_map,
    expansion_offset,
    contraction_linear_map,
    contraction_offset,
    residual_channel_factor,
    readout_layernorm_multiplier,
    readout_layernorm_offset,
    readout_linear_map,
    learner_caption_vectors,
    mentor_caption_vectors,
    mentor_picture_vectors,
    divisor_per_slot,
    active_program_slot,
    matching_caption_slot,
):
    group_count = incoming_feature_maps.shape[0]
    local_width = incoming_feature_maps.shape[3]
    shard_count = lax.axis_size("fsdp")
    shard_index = lax.axis_index("fsdp")
    data_index = lax.axis_index("dp")
    full_width = local_width * shard_count
    token_rows = group_count * SIDE * SIDE
    convolved = depthwise(incoming_feature_maps, spatial_filter_tensor, spatial_filter_offset)
    values = convolved.astype(jnp.float32).reshape(token_rows, local_width)
    totals, squares = lax.psum((jnp.sum(values, 1), jnp.sum(values * values, 1)), "fsdp")
    mean_val = totals / full_width
    spread = squares / full_width - mean_val * mean_val
    gain_part = lax.dynamic_slice_in_dim(
        unit_layernorm_multiplier, shard_index * local_width, local_width
    )
    shift_part = lax.dynamic_slice_in_dim(
        unit_layernorm_offset_vector, shard_index * local_width, local_width
    )
    local_normed = (
        (values - mean_val[:, None]) / jnp.sqrt(spread[:, None] + EPSILON) * gain_part + shift_part
    ).astype(jnp.bfloat16)
    normed = lax.all_gather(local_normed, "fsdp", axis=1, tiled=True)
    preact = (
        jnp.dot(
            normed,
            lax.all_gather(expansion_linear_map, "dp", axis=0, tiled=True),
            preferred_element_type=jnp.float32,
        )
        + expansion_offset
    )
    hidden = jax.nn.gelu(preact, approximate=False).astype(jnp.bfloat16)
    partials = jnp.dot(
        hidden,
        lax.all_gather(contraction_linear_map, "dp", axis=1, tiled=True),
        preferred_element_type=jnp.float32,
    )
    branch = lax.psum_scatter(
        partials.astype(jnp.bfloat16), "fsdp", scatter_dimension=1, tiled=True
    ).astype(jnp.float32)
    residual = incoming_feature_maps.astype(jnp.float32).reshape(token_rows, local_width)
    block_out = (
        (residual + residual_channel_factor * (branch + contraction_offset))
        .astype(jnp.bfloat16)
        .reshape(incoming_feature_maps.shape)
    )
    pooled = jnp.mean(
        block_out.astype(jnp.float32).reshape(group_count, SIDE * SIDE, local_width), 1
    )
    weight_full = readout_linear_map.astype(jnp.float32)
    totals, squares = lax.psum((jnp.sum(pooled, 1), jnp.sum(pooled * pooled, 1)), "fsdp")
    mean_val = totals / full_width
    spread = squares / full_width - mean_val * mean_val
    head_normed = (pooled - mean_val[:, None]) / jnp.sqrt(
        spread[:, None] + EPSILON
    ) * readout_layernorm_multiplier + readout_layernorm_offset
    embedding = lax.psum(jnp.dot(head_normed, weight_full, precision=HIGHEST), "fsdp")
    logit_divisor = lax.dynamic_index_in_dim(
        divisor_per_slot, active_program_slot[0], keepdims=False
    )
    learner_vector_list = unit_rows(embedding)
    mentor_vector_list = unit_rows(mentor_picture_vectors.astype(jnp.float32))
    learner_caption_grid = unit_rows(learner_caption_vectors.astype(jnp.float32))
    mentor_caption_grid = unit_rows(mentor_caption_vectors.astype(jnp.float32))
    per_device = group_count // shard_count
    key_count = learner_caption_vectors.shape[0]
    learner_picture_vectors, mentor_picture_list = (
        lax.all_gather(learner_vector_list, "dp", axis=0, tiled=True),
        lax.all_gather(mentor_vector_list, "dp", axis=0, tiled=True),
    )
    first_column_index = (data_index * shard_count + shard_index) * key_count
    stats = row_stats(
        learner_picture_vectors,
        mentor_picture_list,
        learner_caption_grid,
        mentor_caption_grid,
        matching_caption_slot,
        first_column_index,
        logit_divisor,
    )
    merged = combined_all(stats, ("dp", "fsdp"), combine_stats)
    offset = (data_index * shard_count + shard_index) * per_device
    picked = [lax.dynamic_slice_in_dim(member, offset, per_device, 0) for member in merged]
    log_student = picked[0] + jnp.log(picked[1])
    log_teacher = picked[2] + jnp.log(picked[3])
    losses = picked[4] / picked[3] - log_teacher + 2.0 * log_student - picked[5]
    return (block_out, embedding, losses)


def solution(mesh):
    placed = (
        P("dp", None, None, "fsdp"),
        P(None, None, "fsdp"),
        P("fsdp"),
        P(),
        P(),
        P("dp", "fsdp"),
        P("fsdp"),
        P("fsdp", "dp"),
        P("fsdp"),
        P("fsdp"),
        P("fsdp"),
        P("fsdp"),
        P("fsdp", None),
        P(("dp", "fsdp"), None),
        P(("dp", "fsdp"), None),
        P("dp", None),
        P(),
        P(),
        P(),
    )
    return jax.shard_map(
        on_device,
        mesh=mesh,
        in_specs=placed,
        out_specs=(P("dp", None, None, "fsdp"), P("dp", None), P(("dp", "fsdp"))),
        check_vma=False,
    )
```

profile of v0, /device:TPU:1, one launch (start us, length us, event | category | flops | bytes accessed | tf_op | source)
XLA Modules:
  0.0 862.0 jit_solution(14012165022689869838)
XLA Ops:
  7.2 1.2 convert_reduce_fusion.50
  8.4 1.1 convert_reduce_fusion.49
  9.5 0.9 convert_reduce_fusion.48
  10.5 1.1 convert_element_type.546
  11.5 5.7 convert_reduce_fusion.1
  17.4 0.8 dynamic_slice.47
  18.1 0.8 dynamic_slice.48
  18.9 15.0 %all-reduce.2 = (f32[512]{0:T(512)S(1)}, f32[512]{0:T(512)S(1)}) all-reduce(f32[512]{0:T(512)S(1)} %reduce_sum.124, f32[512]{0:T(512)S(1)} %reduce_sum.122), channel_id=1, replica_groups=mesh['dp'=32,'fsdp'=8] {'fsdp'}, use_global_device_ids=true, to_apply=%region_3.4 | all-reduce | flops 1024 | bytes 8192 | tf_op jit(solution)/shard_map/psum | solution.py:131
  33.9 1.0 fusion.142
  35.0 0.7 all-gather.18.cloned.1.call-update
  35.7 0.7 all-gather.20.cloned.1.call-update
  36.4 0.2 reduce-scatter.4.cloned.1.call-start
  36.6 30.2 %all-gather.16.cloned.1.call-done = bf16[512,3072]{1,0:T(8,128)(2,1)} async-done(((bf16[512,384]{1,0:T(8,128)(2,1)}), bf16[512,3072]{1,0:T(8,128)(2,1)}) %all-gather.16.cloned.1.call-update) | async-done | bytes 3145744 | tf_op jit(solution)/shard_map/all_gather | solution.py:143
  66.8 105.3 %all-gather.18.cloned.1.call-done = bf16[3072,1536]{1,0:T(8,128)(2,1)} async-done(((bf16[96,1536]{1,0:T(8,128)(2,1)}), bf16[3072,1536]{1,0:T(8,128)(2,1)}) %all-gather.18.cloned.1.call-update) | async-done | bytes 9437200 | tf_op jit(solution)/shard_map/all_gather | solution.py:147
  172.1 103.2 %all-gather.20.cloned.1.call-done = bf16[1536,3072]{0,1:T(8,128)(2,1)} async-done(((bf16[1536,96]{0,1:T(8,128)(2,1)}), bf16[1536,3072]{0,1:T(8,128)(2,1)}) %all-gather.20.cloned.1.call-update) | async-done | bytes 9437200 | tf_op jit(solution)/shard_map/all_gather | solution.py:155
  275.3 25.6 %convolution_convert_fusion = bf16[512,3072]{1,0:T(8,128)(2,1)} fusion(bf16[1536,3072]{0,1:T(8,128)(2,1)} %all-gather.20.cloned.1.call-done, bf16[512,3072]{1,0:T(8,128)(2,1)} %all-gather.16.cloned.1.call-done, bf16[3072,1536]{1,0:T(8,128)(2,1)} %all-gather.18.cloned.1.call-done, f32[1536]{0:T(1024)S(1)} %copy-done.12), kind=kOutput, calls=%fused_computation.60 | convolution fusion | flops 9717153792 | bytes 25171968 | tf_op jit(solution)/shard_map/dot_general | solution.py:153
  300.9 4.7 copy.22
  306.4 0.6 dynamic_slice.49
  307.3 38.2 %all_gather.59 = bf16[256,768]{1,0:T(8,128)(2,1)S(1)} all-gather(bf16[8,768]{1,0:T(8,128)(2,1)S(1)} %fusion.154), channel_id=1, replica_groups=mesh['dp'=32,'fsdp'=8] {'dp'}, dimensions={0}, use_global_device_ids=true | all-gather | bytes 405504 | tf_op jit(solution)/shard_map/all_gather | solution.py:189
  345.6 0.9 fusion.200
  346.5 71.3 %all-gather.8 = f32[256,1,256]{2,1,0:T(1,128)S(1)} all-gather(f32[1,1,256]{2,1,0:T(1,128)S(1)} %bitcast.102), channel_id=4, replica_groups=mesh['dp'=32,'fsdp'=8] {'dp','fsdp'}, dimensions={0}, use_global_device_ids=true | all-gather | bytes 263168 | tf_op jit(solution)/shard_map/all_gather | solution.py:15
  417.8 0.2 slice.469
  418.0 0.1 fusion.144
  418.2 1.2 copy.23
  419.4 0.9 convert_reduce_fusion
  420.4 0.1 multiply_reduce_fusion.4
  420.5 11.9 %all-reduce.1 = (f32[8]{0:T(128)S(1)}, f32[8]{0:T(128)S(1)}) all-reduce(f32[8]{0:T(128)S(1)} %get-tuple-element.137, f32[8]{0:T(128)S(1)} %get-tuple-element.136), channel_id=1, replica_groups=mesh['dp'=32,'fsdp'=8] {'fsdp'}, use_global_device_ids=true, to_apply=%region_9.10 | all-reduce | flops 16 | bytes 128 | tf_op jit(solution)/shard_map/psum | solution.py:171
  432.5 0.4 fusion.155
  432.9 22.0 %psum.39 = f32[8,768]{1,0:T(8,128)S(1)} all-reduce(f32[8,768]{1,0:T(8,128)S(1)} %fusion.155), channel_id=1, replica_groups=mesh['dp'=32,'fsdp'=8] {'fsdp'}, use_global_device_ids=true, to_apply=%region_10.11 | all-reduce | flops 6144 | bytes 49152 | tf_op jit(solution)/shard_map/psum | solution.py:177
  455.0 36.0 %all_gather.54 = bf16[256,768]{1,0:T(8,128)(2,1)S(1)} all-gather(bf16[8,768]{1,0:T(8,128)(2,1)S(1)} %divide_convert_fusion), channel_id=1, replica_groups=mesh['dp'=32,'fsdp'=8] {'dp'}, dimensions={0}, use_global_device_ids=true | all-gather | bytes 405504 | tf_op jit(solution)/shard_map/all_gather | solution.py:188
  491.0 0.9 fusion.199
  492.0 75.1 %all-gather.7 = f32[256,1,256]{2,1,0:T(1,128)S(1)} all-gather(f32[1,1,256]{2,1,0:T(1,128)S(1)} %bitcast.107), channel_id=3, replica_groups=mesh['dp'=32,'fsdp'=8] {'dp','fsdp'}, dimensions={0}, use_global_device_ids=true | all-gather | bytes 263168 | tf_op jit(solution)/shard_map/all_gather | solution.py:15
  567.1 0.2 slice.468
  567.3 59.6 %all-gather.9 = f32[256,1,256]{2,1,0:T(1,128)S(1)} all-gather(f32[1,1,256]{2,1,0:T(1,128)S(1)} %bitcast.106), channel_id=5, replica_groups=mesh['dp'=32,'fsdp'=8] {'dp','fsdp'}, dimensions={0}, use_global_device_ids=true | all-gather | bytes 263168 | tf_op jit(solution)/shard_map/all_gather | solution.py:15
  626.9 0.2 slice.470
  627.1 59.6 %all-gather.10 = f32[256,1,256]{2,1,0:T(1,128)S(1)} all-gather(f32[1,1,256]{2,1,0:T(1,128)S(1)} %bitcast.105), channel_id=6, replica_groups=mesh['dp'=32,'fsdp'=8] {'dp','fsdp'}, dimensions={0}, use_global_device_ids=true | all-gather | bytes 263168 | tf_op jit(solution)/shard_map/all_gather | solution.py:15
  686.7 0.2 slice.471
  686.9 59.6 %all-gather.11 = f32[256,1,256]{2,1,0:T(1,128)S(1)} all-gather(f32[1,1,256]{2,1,0:T(1,128)S(1)} %bitcast.104), channel_id=7, replica_groups=mesh['dp'=32,'fsdp'=8] {'dp','fsdp'}, dimensions={0}, use_global_device_ids=true | all-gather | bytes 263168 | tf_op jit(solution)/shard_map/all_gather | solution.py:15
  746.4 0.2 slice.472
  746.6 59.6 %all-gather.6 = f32[256,1,256]{2,1,0:T(1,128)S(1)} all-gather(f32[1,1,256]{2,1,0:T(1,128)S(1)} %bitcast.103), channel_id=2, replica_groups=mesh['dp'=32,'fsdp'=8] {'dp','fsdp'}, dimensions={0}, use_global_device_ids=true | all-gather | bytes 263168 | tf_op jit(solution)/shard_map/all_gather | solution.py:15
  806.2 0.2 slice.467
  806.5 39.6 %while.20 = (s32[]{:T(128)}, f32[256]{0:T(256)S(1)}, f32[256]{0:T(256)S(1)}, f32[256]{0:T(256)S(1)}, f32[256]{0:T(256)S(1)}, /*index=5*/f32[256]{0:T(256)S(1)}, ...) while((s32[]{:T(128)}, f32[256]{0:T(256)S(1)}, ...), condition=%wide.region_22.23_spmd, body=%wide.region_21.22_spmd.sunk | while | flops 4610 | bytes 35985 | solution.py:18
  846.1 0.7 dynamic_slice.55
  846.8 0.6 dynamic_slice.54
  848.1 0.6 dynamic_slice.53
  848.7 0.6 dynamic_slice.52
  849.3 0.6 dynamic_slice.51
  850.6 0.6 dynamic_slice.50
  (2102 shorter events, 27.4 us)
Async XLA Ops:
  7.2 425.3 %copy-start = (bf16[384,768]{1,0:T(8,128)(2,1)S(1)}, bf16[384,768]{1,0:T(8,128)(2,1)}, u32[]{:S(2)}) copy-start(bf16[384,768]{1,0:T(8,128)(2,1)} %param.33) | copy-start | bytes 1769476
  7.2 268.1 %copy-start.12 = (f32[1536]{0:T(1024)S(1)}, f32[1536]{0:T(1024)}, u32[]{:S(2)}) copy-start(f32[1536]{0:T(1024)} %param.27) | copy-start | bytes 18436
  7.2 59.6 %all-gather.16.cloned.1.call-start = ((), (), s32[]{:S(2)}) async-start(), calls=%async_computation.1 | async-start | bytes 3538944 | tf_op jit(solution)/shard_map/all_gather | solution.py:143
  34.9 137.2 %all-gather.18.cloned.1.call-start = ((), (), s32[]{:S(2)}) async-start(), calls=%async_computation.2 | async-start | bytes 9732096 | tf_op jit(solution)/shard_map/all_gather | solution.py:147
  35.7 239.6 %all-gather.20.cloned.1.call-start = ((), (), s32[]{:S(2)}) async-start(), calls=%async_computation.3 | async-start | bytes 9732096 | tf_op jit(solution)/shard_map/all_gather | solution.py:155
  36.4 381.8 %reduce-scatter.4.cloned.1.call-start = ((), (), s32[]{:S(2)}) async-start(), calls=%async_computation.4 | async-start | bytes 3538944
  305.6 0.9 copy-start.13
  305.6 1.5 copy-start.6
  305.6 39.9 %copy-start.4 = (bf16[64,768]{1,0:T(8,128)(2,1)S(1)}, bf16[64,768]{1,0:T(8,128)(2,1)}, u32[]{:S(2)}) copy-start(bf16[64,768]{1,0:T(8,128)(2,1)} %param.35) | copy-start | bytes 294916
  305.6 112.5 %copy-start.5 = (bf16[64,768]{1,0:T(8,128)(2,1)S(1)}, bf16[64,768]{1,0:T(8,128)(2,1)}, u32[]{:S(2)}) copy-start(bf16[64,768]{1,0:T(8,128)(2,1)} %param.34) | copy-start | bytes 294916
  305.6 113.8 %copy-start.1 = (bf16[8,8,8,384]{3,2,1,0:T(8,128)(2,1)S(1)}, bf16[8,8,8,384]{3,2,1,0:T(8,128)(2,1)}, u32[]{:S(2)}) copy-start(bf16[8,8,8,384]{3,2,1,0:T(8,128)(2,1)} %param.21) | copy-start | bytes 1179652
  305.6 113.8 %copy-start.7 = (f32[384]{0:T(512)S(1)}, f32[384]{0:T(512)}, u32[]{:S(2)}) copy-start(f32[384]{0:T(512)} %param.29) | copy-start | bytes 4612
  305.6 113.8 %copy-start.8 = (f32[384]{0:T(512)S(1)}, f32[384]{0:T(512)}, u32[]{:S(2)}) copy-start(f32[384]{0:T(512)} %param.30) | copy-start | bytes 4612
  305.6 126.8 %copy-start.9 = (f32[384]{0:T(512)S(1)}, f32[384]{0:T(512)}, u32[]{:S(2)}) copy-start(f32[384]{0:T(512)} %param.32) | copy-start | bytes 4612
  305.6 126.8 %copy-start.10 = (f32[384]{0:T(512)S(1)}, f32[384]{0:T(512)}, u32[]{:S(2)}) copy-start(f32[384]{0:T(512)} %param.31) | copy-start | bytes 4612
  346.5 145.4 %copy-start.11 = (s32[256]{0:T(256)S(1)}, s32[256]{0:T(256)}, u32[]{:S(2)}) copy-start(s32[256]{0:T(256)} %param.39) | copy-start | bytes 3076
  417.8 149.5 %copy-start.2 = (f32[256,1,256]{2,1,0:T(1,128)}, f32[256,1,256]{2,1,0:T(1,128)S(1)}, u32[]{:S(2)}) copy-start(f32[256,1,256]{2,1,0:T(1,128)S(1)} %all-gather.8) | copy-start | bytes 786436
  454.8 351.6 %copy-start.3 = (f32[8,768]{1,0:T(8,128)}, f32[8,768]{1,0:T(8,128)S(1)}, u32[]{:S(2)}) copy-start(f32[8,768]{1,0:T(8,128)S(1)} %psum.39) | copy-start | bytes 73732
  567.3 239.2 %slice-start = ((f32[256,1,256]{2,1,0:T(1,128)}), f32[1,1,256]{2,1,0:T(1,128)S(1)}, s32[]{:S(2)}) async-start(f32[256,1,256]{2,1,0:T(1,128)} %copy-done.2), calls=%async_computation.5 | async-start | bytes 2048 | tf_op jit(solution)/shard_map/slice | solution.py:16
Sparse Core Ops, SparseCore 0:
  35.1 31.7 all-gather.15
  69.4 102.6 all-gather.17
  174.7 100.5 all-gather.19
  305.7 33.0 reduce-scatter.3
where the time goes:
time: 863 us; the launch traced here: 862 us
  blocking collectives  508 us (59%)
  waiting for transfers between devices  240 us (28%)
  other arithmetic  28.9 us (3%)
  matrix products  27.8 us (3%)
  local copies, waits for them, and re-layouts  23.3 us (3%)
  between operations  20.6 us (2%)
  loops' own time  13.4 us (2%)
    all_gather x6, blocking collectives, combined_all(): pieces = jax.tree.map(lambda part: lax.all_gather(part, axis), value)  385 us
    all_gather x1, waiting for transfers between devices, on_device(): lax.all_gather(expansion_linear_map, 'dp', axis=0, tiled=True)  105 us
    all_gather x1, waiting for transfers between devices, on_device(): lax.all_gather(contraction_linear_map, 'dp', axis=1, tiled=True)  103 us
    all_gather x1, blocking collectives, on_device(): lax.all_gather(mentor_vector_list, 'dp', axis=0, tiled=True)  38.2 us
    all_gather x1, blocking collectives, on_device(): lax.all_gather(learner_vector_list, 'dp', axis=0, tiled=True)  36 us
    all_gather x1, waiting for transfers between devices, on_device(): normed = lax.all_gather(local_normed, 'fsdp', axis=1, tiled=True)  30.2 us
    dot_general x1, matrix products, on_device(): jnp.dot(hidden, lax.all_gather(contraction_linear_map, 'dp', axis=1, tile...  25.6 us
    psum x1, blocking collectives, on_device(): lax.psum(jnp.dot(head_normed, weight_full, precision=HIGHEST), 'fsdp')  22 us
  transfers between devices with their start and end apart: 4, of which 3 were waited for; matrix products, arithmetic and copies ran while one was open for 0% of the time, Pallas kernels for 0%

commit v1 on v0

v1 whole, which is shorter than its diff:
```python
import jax
import jax.numpy as jnp
from jax import lax
from jax.sharding import PartitionSpec as P

SIDE = 8
KERNEL = 7


EPSILON = 1e-06
HIGHEST = lax.Precision.HIGHEST


def depthwise(incoming_feature_maps, spatial_filter_tensor, spatial_filter_offset):
    radius = KERNEL // 2
    padded = jnp.pad(
        incoming_feature_maps.astype(jnp.float32),
        ((0, 0), (radius, radius), (radius, radius), (0, 0)),
    )
    summed = jnp.zeros(incoming_feature_maps.shape, jnp.float32)
    for vertical in range(KERNEL):
        for horizontal in range(KERNEL):
            window = padded[:, vertical : vertical + SIDE, horizontal : horizontal + SIDE, :]
            summed = (
                summed + spatial_filter_tensor[vertical, horizontal].astype(jnp.float32) * window
            )
    return (summed + spatial_filter_offset).astype(jnp.bfloat16)


def unit_rows(values):
    return (values / jnp.sqrt(jnp.sum(values * values, -1, keepdims=True) + EPSILON)).astype(
        jnp.bfloat16
    )


def logits(queries, keys, divisor):
    return (
        lax.dot_general(
            queries, keys, (((1,), (1,)), ((), ())), preferred_element_type=jnp.float32
        )
        / divisor
    )


def broadcast_gather(value, axis):
    copies = jnp.broadcast_to(value[None], (lax.axis_size(axis),) + value.shape)
    return lax.all_to_all(copies, axis, 0, 0)


def split_product(values, weights):
    top = lax.reduce_precision(values, 8, 7)
    rest = values - top
    middle = lax.reduce_precision(rest, 8, 7)
    pieces = jnp.concatenate([top, middle, rest - middle], 0).astype(jnp.bfloat16)
    product = jnp.dot(pieces, weights, preferred_element_type=jnp.float32)
    rows = values.shape[0]
    return product[2 * rows :] + product[rows : 2 * rows] + product[:rows]


def on_device(
    incoming_feature_maps,
    spatial_filter_tensor,
    spatial_filter_offset,
    unit_layernorm_multiplier,
    unit_layernorm_offset_vector,
    expansion_linear_map,
    expansion_offset,
    contraction_linear_map,
    contraction_offset,
    residual_channel_factor,
    readout_layernorm_multiplier,
    readout_layernorm_offset,
    readout_linear_map,
    learner_caption_vectors,
    mentor_caption_vectors,
    mentor_picture_vectors,
    divisor_per_slot,
    active_program_slot,
    matching_caption_slot,
):
    group_count = incoming_feature_maps.shape[0]
    local_width = incoming_feature_maps.shape[3]
    shard_count = lax.axis_size("fsdp")
    shard_index = lax.axis_index("fsdp")
    data_index = lax.axis_index("dp")
    full_width = local_width * shard_count
    token_rows = group_count * SIDE * SIDE
    logit_divisor = lax.dynamic_index_in_dim(
        divisor_per_slot, active_program_slot[0], keepdims=False
    )
    key_count = learner_caption_vectors.shape[0]
    teacher_rows = broadcast_gather(unit_rows(mentor_picture_vectors.astype(jnp.float32)), "dp")
    teacher_part = logits(
        teacher_rows.reshape(-1, teacher_rows.shape[2]),
        unit_rows(mentor_caption_vectors.astype(jnp.float32)),
        logit_divisor,
    )
    teacher = lax.all_to_all(
        teacher_part.reshape(lax.axis_size("dp"), group_count, key_count), "dp", 0, 0
    )
    teacher = jnp.swapaxes(teacher, 0, 1).reshape(group_count, -1)
    top_teacher = jnp.max(teacher, 1, keepdims=True)
    teacher_weights = jnp.exp(teacher - top_teacher)
    sum_teacher = jnp.sum(teacher_weights, 1)
    student_keys = lax.all_gather(
        unit_rows(learner_caption_vectors.astype(jnp.float32)), "dp", axis=0, tiled=True
    )
    readout_full = lax.all_gather(readout_linear_map, "fsdp", axis=0, tiled=True)
    head_params = broadcast_gather(
        jnp.stack([readout_layernorm_multiplier, readout_layernorm_offset]), "fsdp"
    )
    head_gain = head_params[:, 0].reshape(full_width)
    head_shift = head_params[:, 1].reshape(full_width)
    convolved = depthwise(incoming_feature_maps, spatial_filter_tensor, spatial_filter_offset)
    values = convolved.astype(jnp.float32).reshape(token_rows, local_width)
    totals, squares = lax.psum((jnp.sum(values, 1), jnp.sum(values * values, 1)), "fsdp")
    mean_val = totals / full_width
    spread = squares / full_width - mean_val * mean_val
    gain_part = lax.dynamic_slice_in_dim(
        unit_layernorm_multiplier, shard_index * local_width, local_width
    )
    shift_part = lax.dynamic_slice_in_dim(
        unit_layernorm_offset_vector, shard_index * local_width, local_width
    )
    local_normed = (
        (values - mean_val[:, None]) / jnp.sqrt(spread[:, None] + EPSILON) * gain_part + shift_part
    ).astype(jnp.bfloat16)
    normed = lax.all_gather(local_normed, "fsdp", axis=1, tiled=True)
    preact = (
        jnp.dot(
            normed,
            lax.all_gather(expansion_linear_map, "dp", axis=0, tiled=True),
            preferred_element_type=jnp.float32,
        )
        + expansion_offset
    )
    hidden = jax.nn.gelu(preact, approximate=False).astype(jnp.bfloat16)
    partials = jnp.dot(
        hidden,
        lax.all_gather(contraction_linear_map, "dp", axis=1, tiled=True),
        preferred_element_type=jnp.float32,
    )
    branch = lax.psum_scatter(
        partials.astype(jnp.bfloat16), "fsdp", scatter_dimension=1, tiled=True
    ).astype(jnp.float32)
    residual = incoming_feature_maps.astype(jnp.float32).reshape(token_rows, local_width)
    block_out = (
        (residual + residual_channel_factor * (branch + contraction_offset))
        .astype(jnp.bfloat16)
        .reshape(incoming_feature_maps.shape)
    )
    pooled = jnp.mean(
        block_out.astype(jnp.float32).reshape(group_count, SIDE * SIDE, local_width), 1
    )
    pooled_full = broadcast_gather(pooled, "fsdp")
    pooled_full = jnp.swapaxes(pooled_full, 0, 1).reshape(group_count, full_width)
    mean_val = jnp.mean(pooled_full, 1, keepdims=True)
    centered = pooled_full - mean_val
    spread = jnp.mean(centered * centered, 1, keepdims=True)
    head_normed = centered / jnp.sqrt(spread + EPSILON) * head_gain + head_shift
    embedding = split_product(head_normed, readout_full)
    student = logits(unit_rows(embedding), student_keys, logit_divisor)
    local_columns = lax.iota(jnp.int32, student.shape[1])
    column_ids = (
        local_columns // key_count * shard_count + shard_index
    ) * key_count + local_columns % key_count
    labels = lax.dynamic_slice_in_dim(matching_caption_slot, data_index * group_count, group_count)
    top_student = jnp.max(student, 1, keepdims=True)
    sum_student = jnp.sum(jnp.exp(student - top_student), 1)
    label_score = jnp.sum(jnp.where(labels[:, None] == column_ids[None, :], student, 0.0), 1)
    cross_sum = jnp.sum(teacher_weights * (teacher - student), 1)
    stats = jnp.stack(
        [top_student[:, 0], sum_student, top_teacher[:, 0], sum_teacher, cross_sum, label_score], 1
    )
    per_device = group_count // shard_count
    stats = lax.all_to_all(stats.reshape(shard_count, per_device, 6), "fsdp", 0, 0)
    top_s, sum_s, top_t, sum_t, cross, label = [stats[:, :, member] for member in range(6)]
    best_s = jnp.max(top_s, 0)
    best_t = jnp.max(top_t, 0)
    scale_t = jnp.exp(top_t - best_t)
    total_t = jnp.sum(sum_t * scale_t, 0)
    log_student = best_s + jnp.log(jnp.sum(sum_s * jnp.exp(top_s - best_s), 0))
    losses = (
        jnp.sum(cross * scale_t, 0) / total_t
        - (best_t + jnp.log(total_t))
        + 2.0 * log_student
        - jnp.sum(label, 0)
    )
    return (block_out, embedding, losses)


def solution(mesh):
    placed = (
        P("dp", None, None, "fsdp"),
        P(None, None, "fsdp"),
        P("fsdp"),
        P(),
        P(),
        P("dp", "fsdp"),
        P("fsdp"),
        P("fsdp", "dp"),
        P("fsdp"),
        P("fsdp"),
        P("fsdp"),
        P("fsdp"),
        P("fsdp", None),
        P(("dp", "fsdp"), None),
        P(("dp", "fsdp"), None),
        P("dp", None),
        P(),
        P(),
        P(),
    )
    return jax.shard_map(
        on_device,
        mesh=mesh,
        in_specs=placed,
        out_specs=(P("dp", None, None, "fsdp"), P("dp", None), P(("dp", "fsdp"))),
        check_vma=False,
    )
```

time: 863 us -> 489 us (0.57)
  blocking collectives: 508 us -> 28.2 us
  waiting for transfers between devices: 240 us -> 357 us
  starting transfers between devices: 0.34 us -> 22.5 us
  loops' own time: 13.4 us -> 0 us
  local copies, waits for them, and re-layouts: 23.3 us -> 10.5 us
  other arithmetic: 28.9 us -> 18.1 us
    all_gather x8 -> x0, blocking collectives: 459 us -> none  [the longest x6 385 us: combined_all(): pieces = jax.tree.map(lambda part: lax.all_gather(part, axis), value)]
    all_gather x0 -> x2, waiting for transfers between devices: none -> 86.8 us  [the longest x1 74.8 us: on_device(): lax.all_gather(unit_rows(learner_caption_vectors.astype(jnp.float32)), 'd...]
    psum x2 -> x0, blocking collectives: 33.9 us -> none  [the longest x1 22 us: on_device(): lax.psum(jnp.dot(head_normed, weight_full, precision=HIGHEST), 'fsdp')]
    all_to_all x0 -> x4, waiting for transfers between devices: none -> 29.4 us  [the longest x3 20.7 us: broadcast_gather(): return lax.all_to_all(copies, axis, 0, 0)]
    all_to_all x0 -> x4, starting transfers between devices: none -> 22 us  [the longest x3 18.2 us: broadcast_gather(): return lax.all_to_all(copies, axis, 0, 0)]
    add x1021 -> x1, other arithmetic: 16.1 us -> 0.01 us  [on_device(): (local_columns // key_count * shard_count + shard_index) * key_count]
    another operation x1 -> x0, loops' own time: 13.4 us -> none  [combined_all(): lax.scan(lambda so_far, share: (join(so_far, share), None), head, tail)]
    all_to_all x0 -> x1, blocking collectives: none -> 13.2 us  [on_device(): lax.all_to_all(stats.reshape(shard_count, per_device, 6), 'fsdp', 0, 0)]
  transfers between devices with their start and end apart: 4 -> 10, of which waited for: 3 -> 9; matrix products, arithmetic and copies ran while one was open for 0% -> 3% of each run, Pallas kernels for 0% -> 0%
where the time goes in v1:
time: 489 us; the launch traced here: 488 us
  waiting for transfers between devices  357 us (73%)
  matrix products  31.4 us (6%)
  blocking collectives  28.2 us (6%)
  starting transfers between devices  22.5 us (5%)
  between operations  20.7 us (4%)
  other arithmetic  18.1 us (4%)
  local copies, waits for them, and re-layouts  10.5 us (2%)
    all_gather x1, waiting for transfers between devices, on_device(): lax.all_gather(contraction_linear_map, 'dp', axis=1, tiled=True)  105 us
    all_gather x1, waiting for transfers between devices, on_device(): lax.all_gather(expansion_linear_map, 'dp', axis=0, tiled=True)  103 us
    all_gather x1, waiting for transfers between devices, on_device(): lax.all_gather(unit_rows(learner_caption_vectors.astype(jnp.float32)), 'd...  74.8 us
    all_gather x1, waiting for transfers between devices, on_device(): normed = lax.all_gather(local_normed, 'fsdp', axis=1, tiled=True)  30.2 us
    dot_general x1, matrix products, on_device(): jnp.dot(hidden, lax.all_gather(contraction_linear_map, 'dp', axis=1, tile...  23.9 us
    all_to_all x3, waiting for transfers between devices, broadcast_gather(): return lax.all_to_all(copies, axis, 0, 0)  20.7 us
    all_to_all x3, starting transfers between devices, broadcast_gather(): return lax.all_to_all(copies, axis, 0, 0)  18.2 us
    psum x1, blocking collectives, on_device(): lax.psum((jnp.sum(values, 1), jnp.sum(values * values, 1)), 'fsdp')  15 us
  transfers between devices with their start and end apart: 10, of which 9 were waited for; matrix products, arithmetic and copies ran while one was open for 3% of the time, Pallas kernels for 0%

profile of v1, /device:TPU:1, one launch (start us, length us, event | category | flops | bytes accessed | tf_op | source)
XLA Modules:
  0.0 488.2 jit_solution(12552628215812586217)
XLA Ops:
  7.2 1.2 convert_reduce_fusion.50
  8.4 1.1 convert_reduce_fusion.49
  9.5 0.9 convert_reduce_fusion.48
  10.5 1.1 convert_element_type.546
  11.6 5.7 %convert_reduce_fusion.1 = (f32[8,8,8]{2,1,0:T(8,128)S(1)}, f32[8,8,8]{2,1,0:T(8,128)S(1)}, bf16[8,8,8,384]{3,2,1,0:T(8,128)(2,1)S(1)}) fusion(f32[384]{0:T(512)} %param.21, f32[384]{0:T(512)S(1)} %get-tuple-element.55, f32[384]{0:T(512)S(1)} %get-tuple-element.56, f32[384]{0:T(512)S(1)} %get-tuple-element.9, f32[384]{0:T(512)S(1)} %get-tuple-element.10, ...), kind=kLoop, calls=%fused_computation.210 | loop fusion | flops 20249600 | bytes 1260544 | tf_op jit(solution)/shard_map/reduce_sum | solution.py:116
  17.4 0.8 dynamic_slice.13
  18.2 0.8 dynamic_slice.14
  19.0 15.0 %all-reduce.1 = (f32[512]{0:T(512)S(1)}, f32[512]{0:T(512)S(1)}) all-reduce(f32[512]{0:T(512)S(1)} %reduce_sum.162, f32[512]{0:T(512)S(1)} %reduce_sum.160), channel_id=1, replica_groups=mesh['dp'=32,'fsdp'=8] {'fsdp'}, use_global_device_ids=true, to_apply=%region_3.4 | all-reduce | flops 1024 | bytes 8192 | tf_op jit(solution)/shard_map/psum | solution.py:116
  34.0 1.0 fusion.142
  35.1 0.7 all-gather.10.cloned.1.call-update
  35.8 0.7 all-gather.8.cloned.1.call-update
  36.5 0.2 reduce-scatter.4.cloned.1.call-start
  36.7 30.2 %all-gather.6.cloned.1.call-done = bf16[512,3072]{1,0:T(8,128)(2,1)} async-done(((bf16[512,384]{1,0:T(8,128)(2,1)}), bf16[512,3072]{1,0:T(8,128)(2,1)}) %all-gather.6.cloned.1.call-update) | async-done | bytes 3145744 | tf_op jit(solution)/shard_map/all_gather | solution.py:128
  66.9 105.3 %all-gather.10.cloned.1.call-done = bf16[1536,3072]{0,1:T(8,128)(2,1)} async-done(((bf16[1536,96]{0,1:T(8,128)(2,1)}), bf16[1536,3072]{0,1:T(8,128)(2,1)}) %all-gather.10.cloned.1.call-update) | async-done | bytes 9437200 | tf_op jit(solution)/shard_map/all_gather | solution.py:140
  172.2 103.2 %all-gather.8.cloned.1.call-done = bf16[3072,1536]{1,0:T(8,128)(2,1)} async-done(((bf16[96,1536]{1,0:T(8,128)(2,1)}), bf16[3072,1536]{1,0:T(8,128)(2,1)}) %all-gather.8.cloned.1.call-update) | async-done | bytes 9437200 | tf_op jit(solution)/shard_map/all_gather | solution.py:132
  275.4 23.9 %convolution_convert_fusion = bf16[512,3072]{1,0:T(8,128)(2,1)S(1)} fusion(bf16[1536,3072]{0,1:T(8,128)(2,1)} %all-gather.10.cloned.1.call-done, bf16[512,3072]{1,0:T(8,128)(2,1)} %all-gather.6.cloned.1.call-done, bf16[3072,1536]{1,0:T(8,128)(2,1)} %all-gather.8.cloned.1.call-done, f32[1536]{0:T(1024)S(1)} %copy-done.9), kind=kOutput, calls=%fused_computation.49 | convolution fusion | flops 9717153792 | bytes 25171968 | tf_op jit(solution)/shard_map/dot_general | solution.py:138
  299.3 2.9 copy.37
  302.4 0.5 all-gather.12.cloned.1.call-update
  303.2 0.7 fusion.146
  304.2 0.8 broadcast_in_dim.16
  305.0 5.3 %all-to-all-start.2 = ((bf16[32,8,768]{2,1,0:T(8,128)(2,1)}), bf16[32,8,768]{2,1,0:T(8,128)(2,1)S(1)}, u32[]{:S(2)}, u32[]{:S(2)}) async-start(bf16[32,8,768]{2,1,0:T(8,128)(2,1)} %broadcast_in_dim.16), calls=%async_computation.2 | async-start | bytes 786432 | tf_op jit(solution)/shard_map/all_to_all | solution.py:47
  311.1 0.6 dynamic_slice.15
  311.9 11.8 %all-to-all-done.2 = bf16[32,8,768]{2,1,0:T(8,128)(2,1)S(1)} async-done(((bf16[32,8,768]{2,1,0:T(8,128)(2,1)}), bf16[32,8,768]{2,1,0:T(8,128)(2,1)S(1)}, u32[]{:S(2)}, u32[]{:S(2)}) %all-to-all-start.2) | async-done | bytes 393248 | tf_op jit(solution)/shard_map/all_to_all | solution.py:47
  323.7 0.6 broadcast_in_dim.14
  324.3 7.4 %all-to-all-start.1 = ((f32[8,2,384]{2,1,0:T(2,128)}), f32[8,2,384]{2,1,0:T(2,128)S(1)}, u32[]{:S(2)}, u32[]{:S(2)}) async-start(f32[8,2,384]{2,1,0:T(2,128)} %broadcast_in_dim.14), calls=%async_computation.1 | async-start | bytes 49152 | tf_op jit(solution)/shard_map/all_to_all | solution.py:47
  331.7 0.9 convolution_divide_fusion.1
  332.7 0.8 reshape.683
  333.5 2.9 all-to-all-done.1
  336.4 3.9 all-to-all-start.3
  340.3 8.8 %all-to-all-done.3 = f32[32,1,512]{2,1,0:T(1,128)S(1)} async-done(((f32[32,1,512]{2,1,0:T(1,128)}), f32[32,1,512]{2,1,0:T(1,128)S(1)}, u32[]{:S(2)}, u32[]{:S(2)}) %all-to-all-start.3) | async-done | bytes 65568 | tf_op jit(solution)/shard_map/all_to_all | solution.py:98
  349.1 0.5 broadcast.242
  349.6 0.8 reduce.118
  350.5 0.2 reduce_max.37
  350.8 1.2 copy.38
  352.1 0.9 convert_reduce_fusion
  353.0 0.6 broadcast_in_dim.13
  353.6 5.5 %all-to-all-start = ((f32[8,8,384]{2,1,0:T(8,128)}), f32[8,8,384]{2,1,0:T(8,128)S(1)}, u32[]{:S(2)}, u32[]{:S(2)}) async-start(f32[8,8,384]{2,1,0:T(8,128)} %broadcast_in_dim.13), calls=%async_computation | async-start | bytes 196608 | tf_op jit(solution)/shard_map/all_to_all | solution.py:47
  359.1 0.2 exponential_reduce_fusion
  359.3 5.9 %all-to-all-done = f32[8,8,384]{2,1,0:T(8,128)S(1)} async-done(((f32[8,8,384]{2,1,0:T(8,128)}), f32[8,8,384]{2,1,0:T(8,128)S(1)}, u32[]{:S(2)}, u32[]{:S(2)}) %all-to-all-start) | async-done | bytes 98336 | tf_op jit(solution)/shard_map/all_to_all | solution.py:47
  365.4 0.2 fusion.158
  365.7 12.0 %all-gather.12.cloned.1.call-done = bf16[3072,768]{1,0:T(8,128)(2,1)} async-done(((bf16[384,768]{1,0:T(8,128)(2,1)}), bf16[3072,768]{1,0:T(8,128)(2,1)}) %all-gather.12.cloned.1.call-update) | async-done | bytes 4718608 | tf_op jit(solution)/shard_map/all_gather | solution.py:108
  377.7 3.1 fusion.149
  380.9 74.8 %all-gather.14.cloned.1.call-done = bf16[2048,768]{1,0:T(8,128)(2,1)} async-done(((bf16[64,768]{1,0:T(8,128)(2,1)}), bf16[2048,768]{1,0:T(8,128)(2,1)}) %all-gather.14.cloned.1.call-update) | async-done | bytes 3145744 | tf_op jit(solution)/shard_map/all_gather | solution.py:105
  455.7 3.6 fusion.211
  459.3 0.2 select_reduce_fusion
  459.6 13.2 %all_to_all.25 = f32[8,1,6]{2,1,0:T(1,128)S(1)} all-to-all(f32[8,1,6]{2,1,0:T(1,128)S(1)} %copy.34), channel_id=1, replica_groups=mesh['dp'=32,'fsdp'=8] {'fsdp'}, dimensions={0} | all-to-all | bytes 384 | tf_op jit(solution)/shard_map/all_to_all | solution.py:176
  472.9 0.8 slice_reduce_fusion.1
  473.6 2.1 slice_reduce_fusion
  (63 shorter events, 2.1 us)
Async XLA Ops:
  7.2 268.2 %copy-start.9 = (f32[1536]{0:T(1024)S(1)}, f32[1536]{0:T(1024)}, u32[]{:S(2)}) copy-start(f32[1536]{0:T(1024)} %param.25) | copy-start | bytes 18436
  7.2 59.7 %all-gather.6.cloned.1.call-start = ((), (), s32[]{:S(2)}) async-start(), calls=%async_computation.6 | async-start | bytes 3538944 | tf_op jit(solution)/shard_map/all_gather | solution.py:128
  35.0 137.2 %all-gather.10.cloned.1.call-start = ((), (), s32[]{:S(2)}) async-start(), calls=%async_computation.8 | async-start | bytes 9732096 | tf_op jit(solution)/shard_map/all_gather | solution.py:140
  35.8 239.6 %all-gather.8.cloned.1.call-start = ((), (), s32[]{:S(2)}) async-start(), calls=%async_computation.7 | async-start | bytes 9732096 | tf_op jit(solution)/shard_map/all_gather | solution.py:132
  36.5 314.3 %reduce-scatter.4.cloned.1.call-start = ((), (), s32[]{:S(2)}) async-start(), calls=%async_computation.11 | async-start | bytes 3538944
  302.2 0.9 copy-start.1
  302.2 1.8 copy-start.4
  302.2 8.1 %copy-start.7 = (f32[384]{0:T(512)S(1)}, f32[384]{0:T(512)}, u32[]{:S(2)}) copy-start(f32[384]{0:T(512)} %param.29) | copy-start | bytes 4612
  302.2 8.2 %copy-start.8 = (f32[384]{0:T(512)S(1)}, f32[384]{0:T(512)}, u32[]{:S(2)}) copy-start(f32[384]{0:T(512)} %param.30) | copy-start | bytes 4612
  302.2 8.8 %copy-start.11 = (f32[64]{0:T(128)S(1)}, f32[64]{0:T(128)}, u32[]{:S(2)}) copy-start(f32[64]{0:T(128)} %param.35) | copy-start | bytes 772
  302.2 9.4 %copy-start.10 = (s32[256]{0:T(256)S(1)}, s32[256]{0:T(256)}, u32[]{:S(2)}) copy-start(s32[256]{0:T(256)} %param.37) | copy-start | bytes 3076
  302.3 9.5 %copy-start.3 = (bf16[64,768]{1,0:T(8,128)(2,1)S(1)}, bf16[64,768]{1,0:T(8,128)(2,1)}, u32[]{:S(2)}) copy-start(bf16[64,768]{1,0:T(8,128)(2,1)} %param.33) | copy-start | bytes 294916
  302.3 49.8 %copy-start = (bf16[8,8,8,384]{3,2,1,0:T(8,128)(2,1)S(1)}, bf16[8,8,8,384]{3,2,1,0:T(8,128)(2,1)}, u32[]{:S(2)}) copy-start(bf16[8,8,8,384]{3,2,1,0:T(8,128)(2,1)} %param.19) | copy-start | bytes 1179652
  302.3 49.8 %copy-start.5 = (f32[384]{0:T(512)S(1)}, f32[384]{0:T(512)}, u32[]{:S(2)}) copy-start(f32[384]{0:T(512)} %param.27) | copy-start | bytes 4612
  302.3 49.7 %copy-start.6 = (f32[384]{0:T(512)S(1)}, f32[384]{0:T(512)}, u32[]{:S(2)}) copy-start(f32[384]{0:T(512)} %param.28) | copy-start | bytes 4612
  302.3 75.4 %all-gather.12.cloned.1.call-start = ((), (), s32[]{:S(2)}) async-start(), calls=%async_computation.9 | async-start | bytes 5308416 | tf_op jit(solution)/shard_map/all_gather | solution.py:108
  302.9 152.8 %all-gather.14.cloned.1.call-start = ((), (), s32[]{:S(2)}) async-start(), calls=%async_computation.10 | async-start | bytes 3244032 | tf_op jit(solution)/shard_map/all_gather | solution.py:105
  305.0 18.7 %all-to-all-start.2 = ((bf16[32,8,768]{2,1,0:T(8,128)(2,1)}), bf16[32,8,768]{2,1,0:T(8,128)(2,1)S(1)}, u32[]{:S(2)}, u32[]{:S(2)}) async-start(bf16[32,8,768]{2,1,0:T(8,128)(2,1)} %broadcast_in_dim.16), calls=%async_computation.2 | async-start | bytes 786432 | tf_op jit(solution)/shard_map/all_to_all | solution.py:47
  324.3 12.1 %all-to-all-start.1 = ((f32[8,2,384]{2,1,0:T(2,128)}), f32[8,2,384]{2,1,0:T(2,128)S(1)}, u32[]{:S(2)}, u32[]{:S(2)}) async-start(f32[8,2,384]{2,1,0:T(2,128)} %broadcast_in_dim.14), calls=%async_computation.1 | async-start | bytes 49152 | tf_op jit(solution)/shard_map/all_to_all | solution.py:47
  336.4 12.7 %all-to-all-start.3 = ((f32[32,1,512]{2,1,0:T(1,128)}), f32[32,1,512]{2,1,0:T(1,128)S(1)}, u32[]{:S(2)}, u32[]{:S(2)}) async-start(f32[32,1,512]{2,1,0:T(1,128)} %reshape.683), calls=%async_computation.3 | async-start | bytes 131072 | tf_op jit(solution)/shard_map/all_to_all | solution.py:98
  353.6 11.6 %all-to-all-start = ((f32[8,8,384]{2,1,0:T(8,128)}), f32[8,8,384]{2,1,0:T(8,128)S(1)}, u32[]{:S(2)}, u32[]{:S(2)}) async-start(f32[8,8,384]{2,1,0:T(8,128)} %broadcast_in_dim.13), calls=%async_computation | async-start | bytes 196608 | tf_op jit(solution)/shard_map/all_to_all | solution.py:47
  380.9 99.4 %copy-start.2 = (f32[8,768]{1,0:T(8,128)}, f32[8,768]{1,0:T(8,128)S(1)}, u32[]{:S(2)}) copy-start(f32[8,768]{1,0:T(8,128)S(1)} %get-tuple-element.66) | copy-start | bytes 73732
Sparse Core Ops, SparseCore 0:
  35.1 31.7 all-gather.5
  69.5 102.6 all-gather.9
  174.8 100.5 all-gather.7
  302.4 33.3 reduce-scatter.3
  337.5 40.1 all-gather.11
  380.2 75.4 all-gather.13
